TPU v7x, 256 devices: a whole 4x4x8 slice. The times are simulated.
256 devices in a mesh: group: 2 (over z_hi), dp: 8 (over x, core), tensor: 16 (over z_lo, y).
Axes of the slice: x: 4, y: 4, z: 8 (z_hi: 2, z_lo: 4; z = z_hi * 4 + z_lo), core: 2. Of those that a mesh axis runs over, the one named last changes fastest.
Arguments:
- teacher_hidden: bfloat16 [4096, 8192], P(('group', 'dp'), 'tensor'), may hold values from -6 to 6
- teacher_gain: float32 [8192], P('tensor'), may hold values from 0.1 to 1.9
- project_weight: bfloat16 [8192, 3584], P('tensor'), may hold values from -0.0625 to 0.0625
- student_hidden: bfloat16 [4096, 3584], P(('group', 'dp', 'tensor')), may hold values from -6 to 6
- student_gain: float32 [3584], replicated, may hold values from 0.1 to 1.9
- gate_weight: bfloat16 [3584, 9472], P(('group', 'dp'), 'tensor'), may hold values from -0.09375 to 0.09375
- up_weight: bfloat16 [3584, 9472], P(('group', 'dp'), 'tensor'), may hold values from -0.09375 to 0.09375
- down_weight: bfloat16 [9472, 3584], P('tensor', ('group', 'dp')), may hold values from -0.0625 to 0.0625
- owner_map: int32 [256, 1], P(('group', 'dp')), may hold values from 0 to 15; in each aligned block of 16 rows (0 to 15, 16 to 31, ...) at most 2 rows name the same one
- token_ids: int32 [4096], P(('group', 'dp', 'tensor')), may hold values from 0 to 511
- token_counts: int32 [256], P(('group', 'dp')), may hold values from 1 to 16
- id_weight: float32 [512], replicated, may hold values from 0.25 to 4
Outputs:
- student_out: bfloat16 [16, 16, 32, 3584], P(('group', 'dp'), 'tensor')
- down_grad: float32 [3584, 9472], P(('group', 'dp'), 'tensor')
Inputs may be any that keep to these rules, and one draw needn't show every extreme that they name: `owner_map`: of the 16 episodes of one index of group and dp (aligned blocks of 16 rows), at most 2 have the same owner; owner o is index o of group and dp in mesh order.
All inputs are finite; a program needn't handle non-finite values.
Results may differ from a plain program's by a relative error of at most 0.02.
Values may be sent and summed in bfloat16 or wider, within the bound.
No kernel may reach another device: no remote copies, remote signals or barrier semaphores. Data moves between devices by JAX's collectives and lax.ppermute only.
A program may use at most 128 MiB of HBM per device.

v0:
```python
import math
import jax
import jax.numpy as jnp
from jax import lax
from jax.sharding import Mesh
from jax.sharding import PartitionSpec as P

DT = 8192
EP_LEN = 16
TENSOR = ("tensor_0", "tensor_1")
OWNERS = ("group", "dp")
GROUP_DP_TENSOR = ("group", "dp", "tensor_0", "tensor_1")
EPSILON = 1e-06


def build_selector(owner_local, owners, capacity):
    owner = owner_local[:, 0]
    index = jnp.arange(owner.shape[0], dtype=jnp.int32)
    earlier = (owner[None, :] == owner[:, None]) & (index[None, :] < index[:, None])
    target = owner * capacity + jnp.sum(earlier.astype(jnp.int32), axis=1)
    slots = jnp.arange(owners * capacity, dtype=jnp.int32)
    return (target[None, :] == slots[:, None]).astype(jnp.bfloat16)


def local(
    teacher_hidden,
    teacher_gain,
    project_weight,
    student_hidden,
    student_gain,
    gate_weight,
    up_weight,
    down_weight,
    owner_map,
    token_ids,
    token_counts,
    id_weight,
):
    owners = lax.axis_size(OWNERS)
    episodes = token_counts.shape[0]
    capacity = max(2, 2 * episodes // owners)
    hidden = gate_weight.shape[1]
    position = lax.axis_index(TENSOR)
    tokens_all = EP_LEN * episodes * owners
    student = student_hidden.astype(jnp.float32)
    rescale = lax.rsqrt(jnp.mean(student * student, axis=1, keepdims=True) + EPSILON)
    normed = (student * rescale * student_gain[None, :]).astype(jnp.bfloat16)
    gathered = lax.all_gather(normed, TENSOR, axis=0, tiled=True)
    both = lax.all_gather(
        jnp.concatenate([gate_weight, up_weight], axis=1), OWNERS, axis=0, tiled=True
    )
    down = lax.all_gather(down_weight, OWNERS, axis=1, tiled=True)
    widened = teacher_hidden.astype(jnp.float32)
    squares = jnp.sum(widened * widened, axis=1)
    scaled = (widened * teacher_gain[None, :]).astype(jnp.bfloat16)
    totals = lax.psum_scatter(squares, TENSOR, scatter_dimension=0, tiled=True)
    inverse = lax.rsqrt(totals / DT + EPSILON)
    summed = lax.psum_scatter(
        jnp.dot(scaled, project_weight, preferred_element_type=jnp.float32).astype(jnp.bfloat16),
        TENSOR,
        scatter_dimension=0,
        tiled=True,
    ).astype(jnp.float32)
    projected = (summed * inverse[:, None]).astype(jnp.bfloat16).astype(jnp.float32)
    sums = jnp.dot(gathered, both, preferred_element_type=jnp.float32)
    activated = (jax.nn.silu(sums[:, :hidden]) * sums[:, hidden:]).astype(jnp.bfloat16)
    branch = jnp.dot(activated, down, preferred_element_type=jnp.float32).astype(jnp.bfloat16)
    branch_local = lax.psum_scatter(branch, TENSOR, scatter_dimension=0, tiled=True)
    predicted = student + branch_local.astype(jnp.float32)
    ids = jnp.arange(id_weight.shape[0], dtype=jnp.int32)
    looked = jnp.sum(jnp.where(token_ids[:, None] == ids[None, :], id_weight[None, :], 0.0), axis=1)
    weight = jnp.where(position < token_counts, looked, 0.0).astype(jnp.bfloat16)
    scale = 1.0 / math.sqrt(tokens_all)
    grad = (weight.astype(jnp.float32)[:, None] * (predicted - projected) * scale).astype(
        jnp.bfloat16
    )
    grad_all = lax.all_gather(grad, TENSOR, axis=0, tiled=True)
    down_grad = lax.psum_scatter(
        jnp.einsum("rc,rh->ch", grad_all, activated, preferred_element_type=jnp.float32).astype(
            jnp.bfloat16
        ),
        OWNERS,
        scatter_dimension=0,
        tiled=True,
    ).astype(jnp.float32)
    selector = build_selector(owner_map, owners, capacity)
    sent = jnp.dot(
        selector, predicted.astype(jnp.bfloat16), preferred_element_type=jnp.float32
    ).astype(jnp.bfloat16)
    student_out = lax.all_to_all(sent, OWNERS, 0, 0, tiled=True)
    return (student_out[None, None], down_grad)


def solution(mesh):
    split = Mesh(
        mesh.devices.reshape(mesh.shape["group"], mesh.shape["dp"], 4, 4),
        ("group", "dp", "tensor_0", "tensor_1"),
    )
    placed = (
        P(OWNERS, TENSOR),
        P(TENSOR),
        P(TENSOR, None),
        P(GROUP_DP_TENSOR, None),
        P(),
        P(OWNERS, TENSOR),
        P(OWNERS, TENSOR),
        P(TENSOR, OWNERS),
        P(OWNERS, None),
        P(GROUP_DP_TENSOR),
        P(OWNERS),
        P(),
    )
    return jax.shard_map(
        local,
        mesh=split,
        in_specs=placed,
        out_specs=(P(OWNERS, TENSOR, None, None), P(OWNERS, TENSOR)),
        check_vma=False,
    )
```

profile of v0, /device:TPU:8, one launch (start us, length us, event | category | flops | bytes accessed | tf_op | source)
XLA Modules:
  0.0 661.9 jit_solution(17144854641354540357)
XLA Ops:
  7.2 1.1 fusion.5
  8.3 1.6 fusion.7
  10.0 2.0 pad_maximum_fusion
  12.1 0.7 all-gather.9.cloned.1.call-update
  12.9 4.4 convolution_convert_fusion.2
  17.3 78.6 %all-gather.5.cloned.1.call-done = bf16[256,3584]{1,0:T(8,128)(2,1)} async-done(((bf16[16,3584]{1,0:T(8,128)(2,1)}), bf16[256,3584]{1,0:T(8,128)(2,1)}) %all-gather.5.cloned.1.call-update) | async-done | bytes 1835024 | tf_op jit(solution)/shard_map/all_gather | solution.py:48
  96.0 112.9 %all-gather.7.cloned.1.call-done = bf16[3584,1184]{1,0:T(8,128)(2,1)} async-done(((bf16[224,1184]{1,0:T(8,128)(2,1)}), bf16[3584,1184]{1,0:T(8,128)(2,1)}) %all-gather.7.cloned.1.call-update) | async-done | bytes 8486928 | tf_op jit(solution)/shard_map/all_gather | solution.py:49
  208.9 7.8 %fusion.16 = f32[256,1184]{0,1:T(8,128)S(1)} fusion(bf16[256,3584]{1,0:T(8,128)(2,1)} %all-gather.5.cloned.1.call-done, bf16[3584,1184]{1,0:T(8,128)(2,1)} %all-gather.7.cloned.1.call-done), kind=kOutput, calls=%fused_computation.36 | convolution fusion | flops 2172649472 | bytes 11534336 | tf_op jit(solution)/shard_map/dot_general | solution.py:65
  216.9 72.3 %all-gather.9.cloned.1.call-done = bf16[592,3584]{0,1:T(8,128)(2,1)} async-done(((bf16[592,224]{0,1:T(8,128)(2,1)}), bf16[592,3584]{0,1:T(8,128)(2,1)}) %all-gather.9.cloned.1.call-update) | async-done | bytes 4243472 | tf_op jit(solution)/shard_map/all_gather | solution.py:52
  289.1 5.2 convolution_convert_fusion.1
  294.4 0.6 copy-done.8
  295.0 0.6 dynamic-slice
  296.4 38.3 %all-reduce = f32[256]{0:T(256)S(1)} all-reduce(f32[256]{0:T(256)S(1)} %fusion.2), channel_id=4, replica_groups=mesh['group'=2,'dp'=8,'tensor_0'=4,'tensor_1'=4] {'tensor_0','tensor_1'}, use_global_device_ids=true, to_apply=%region_6.7.clone | all-reduce | flops 256 | bytes 2048
  335.0 35.2 %reduce-scatter.6.cloned.1.call-done = bf16[16,3584]{1,0:T(8,128)(2,1)} async-done(((bf16[256,3584]{1,0:T(8,128)(2,1)}), bf16[16,3584]{1,0:T(8,128)(2,1)}) %reduce-scatter.6.cloned.1.call-update) | async-done | bytes 114704 | tf_op jit(solution)/shard_map/reduce_scatter | solution.py:58
  370.2 86.1 %reduce-scatter.4.cloned.1.call-done = bf16[16,3584]{1,0:T(8,128)(2,1)} async-done(((bf16[256,3584]{1,0:T(8,128)(2,1)}), bf16[16,3584]{1,0:T(8,128)(2,1)}) %reduce-scatter.4.cloned.1.call-update) | async-done | bytes 114704 | tf_op jit(solution)/shard_map/reduce_scatter | solution.py:68
  456.3 1.7 multiply_convert_fusion
  458.1 83.8 %all-gather.11.cloned.1.call-done = bf16[256,3584]{1,0:T(8,128)(2,1)} async-done(((bf16[16,3584]{1,0:T(8,128)(2,1)}), bf16[256,3584]{1,0:T(8,128)(2,1)}) %all-gather.11.cloned.1.call-update) | async-done | bytes 1835024 | tf_op jit(solution)/shard_map/all_gather | solution.py:77
  541.8 5.2 convolution_convert_fusion
  547.1 0.6 copy-done.7
  548.0 0.2 convolution_convert_fusion.3
  548.3 18.0 %all_to_all.9 = bf16[16,2,3584]{2,1,0:T(2,128)(2,1)S(1)} all-to-all(bf16[16,2,3584]{2,1,0:T(2,128)(2,1)S(1)} %all_to_all.6), channel_id=1, replica_groups=mesh['group'=2,'dp'=8,'tensor_0'=4,'tensor_1'=4] {'group','dp'}, dimensions={0} | all-to-all | bytes 458752 | tf_op jit(solution)/shard_map/all_to_all | solution.py:90
  566.3 0.8 broadcast_in_dim.18
  567.1 86.2 %reduce-scatter.8.cloned.1.call-done = bf16[224,592]{1,0:T(8,128)(2,1)} async-done(((bf16[3584,592]{1,0:T(8,128)(2,1)}), bf16[224,592]{1,0:T(8,128)(2,1)}) %reduce-scatter.8.cloned.1.call-update) | async-done | bytes 265232 | tf_op jit(solution)/shard_map/reduce_scatter | solution.py:78
  653.2 1.8 convert_element_type.76
  (38 shorter events, 1.4 us)
Async XLA Ops:
  7.2 5.7 copy-start.1
  7.2 5.7 copy-start.3
  7.2 88.8 %all-gather.5.cloned.1.call-start = ((), (), s32[]{:S(2)}) async-start(), calls=%async_computation.4 | async-start | bytes 1949696 | tf_op jit(solution)/shard_map/all_gather | solution.py:48
  10.0 198.9 %all-gather.7.cloned.1.call-start = ((), (), s32[]{:S(2)}) async-start(), calls=%async_computation.5 | async-start | bytes 9748480 | tf_op jit(solution)/shard_map/all_gather | solution.py:49
  12.1 277.1 %all-gather.9.cloned.1.call-start = ((), (), s32[]{:S(2)}) async-start(), calls=%async_computation.6 | async-start | bytes 4874240 | tf_op jit(solution)/shard_map/all_gather | solution.py:52
  12.8 357.4 %reduce-scatter.6.cloned.1.call-start = ((), (), s32[]{:S(2)}) async-start(), calls=%async_computation.8 | async-start | bytes 1949696 | tf_op jit(solution)/shard_map/reduce_scatter | solution.py:58
  17.3 439.0 %reduce-scatter.4.cloned.1.call-start = ((), (), s32[]{:S(2)}) async-start(), calls=%async_computation.7 | async-start | bytes 1949696 | tf_op jit(solution)/shard_map/reduce_scatter | solution.py:68
  294.3 0.7 copy-start.8
  294.3 40.5 %copy-start.4 = (f32[512]{0:T(512)S(1)}, f32[512]{0:T(512)}, u32[]{:S(2)}) copy-start(f32[512]{0:T(512)} %param.23) | copy-start | bytes 6148
  294.3 40.5 %copy-start.5 = (s32[16]{0:T(128)S(1)}, s32[16]{0:T(128)}, u32[]{:S(2)}) copy-start(s32[16]{0:T(128)} %param.21) | copy-start | bytes 196
  294.3 40.7 %copy-start.6 = (s32[16]{0:T(128)S(1)}, s32[16]{0:T(128)}, u32[]{:S(2)}) copy-start(s32[16]{0:T(128)} %param.22) | copy-start | bytes 196
  294.4 161.9 %copy-start = (bf16[16,3584]{1,0:T(8,128)(2,1)S(1)}, bf16[16,3584]{1,0:T(8,128)(2,1)}, u32[]{:S(2)}) copy-start(bf16[16,3584]{1,0:T(8,128)(2,1)} %param.15) | copy-start | bytes 344068
  294.4 247.4 %all-gather.11.cloned.1.call-start = ((), (), s32[]{:S(2)}) async-start(), calls=%async_computation.9 | async-start | bytes 1949696 | tf_op jit(solution)/shard_map/all_gather | solution.py:77
  458.0 195.2 %reduce-scatter.8.cloned.1.call-start = ((), (), s32[]{:S(2)}) async-start(), calls=%async_computation.10 | async-start | bytes 4874240 | tf_op jit(solution)/shard_map/reduce_scatter | solution.py:78
  547.0 0.7 copy-start.7
  547.0 0.9 copy-start.2
Sparse Core Ops, SparseCore 0:
  10.4 85.5 all-gather.4
  99.3 109.5 all-gather.6
  211.6 77.4 all-gather.8
  291.5 78.5 reduce-scatter.5
  372.7 83.4 reduce-scatter.3
  458.5 83.3 all-gather.10
  547.2 106.0 reduce-scatter.7
where the time goes:
time: 662 us
  waiting for transfers between devices  556 us (84%)
  blocking collectives  56.4 us (9%)
  matrix products  22.8 us (3%)
  between operations  14.9 us (2%)
  other arithmetic  9.05 us (1%)
    all_gather x1, waiting for transfers between devices, local(): lax.all_gather(jnp.concatenate([gate_weight, up_weight], axis=1), OWNERS,...  113 us
    reduce_scatter x1, waiting for transfers between devices, local(): lax.psum_scatter(jnp.einsum('rc,rh->ch', grad_all, activated, preferred_e...  86.2 us
    reduce_scatter x1, waiting for transfers between devices, local(): lax.psum_scatter(branch, TENSOR, scatter_dimension=0, tiled=True)  86.1 us
    all_gather x1, waiting for transfers between devices, local(): grad_all = lax.all_gather(grad, TENSOR, axis=0, tiled=True)  83.8 us
    all_gather x1, waiting for transfers between devices, local(): gathered = lax.all_gather(normed, TENSOR, axis=0, tiled=True)  78.6 us
    all_gather x1, waiting for transfers between devices, local(): down = lax.all_gather(down_weight, OWNERS, axis=1, tiled=True)  72.3 us
    unnamed x1, blocking collectives  38.3 us
    reduce_scatter x1, waiting for transfers between devices, local(): lax.psum_scatter(jnp.dot(scaled, project_weight, preferred_element_type=j...  35.2 us
  transfers between devices with their start and end apart: 7, of which 7 were waited for; matrix products, arithmetic and copies ran while one was open for 3% of the time, Pallas kernels for 0%

commit v1 on v0

--- a/solution.py
+++ b/solution.py
@@ -74,7 +74,9 @@
     grad = (weight.astype(jnp.float32)[:, None] * (predicted - projected) * scale).astype(
         jnp.bfloat16
     )
-    grad_all = lax.all_gather(grad, TENSOR, axis=0, tiled=True)
+    grad_all = jnp.concatenate(
+        lax.all_to_all(jnp.stack([grad] * lax.axis_size(TENSOR)), TENSOR, 0, 0), axis=0
+    )
     down_grad = lax.psum_scatter(
         jnp.einsum("rc,rh->ch", grad_all, activated, preferred_element_type=jnp.float32).astype(
             jnp.bfloat16

time: 662 us -> 618 us (0.934)
  waiting for transfers between devices: 556 us -> 471 us
  blocking collectives: 56.4 us -> 97.9 us
    all_gather x1 -> x0, waiting for transfers between devices: 83.8 us -> none  [local(): grad_all = lax.all_gather(grad, TENSOR, axis=0, tiled=True)]
    all_to_all x0 -> x1, blocking collectives: none -> 39.9 us  [local(): lax.all_to_all(jnp.stack([grad] * lax.axis_size(TENSOR)), TENSOR, 0, 0)]
  transfers between devices with their start and end apart: 7 -> 6, of which waited for: 7 -> 6; matrix products, arithmetic and copies ran while one was open for 3% -> 4% of each run, Pallas kernels for 0% -> 0%
where the time goes in v1:
time: 618 us; the launch traced here: 617 us
  waiting for transfers between devices  471 us (76%)
  blocking collectives  97.9 us (16%)
  matrix products  21.3 us (3%)
  between operations  14.9 us (2%)
  other arithmetic  8.41 us (1%)
    all_gather x1, waiting for transfers between devices, local(): lax.all_gather(jnp.concatenate([gate_weight, up_weight], axis=1), OWNERS,...  113 us
    reduce_scatter x1, waiting for transfers between devices, local(): lax.psum_scatter(branch, TENSOR, scatter_dimension=0, tiled=True)  86 us
    reduce_scatter x1, waiting for transfers between devices, local(): lax.psum_scatter(jnp.einsum('rc,rh->ch', grad_all, activated, preferred_e...  85.7 us
    all_gather x1, waiting for transfers between devices, local(): gathered = lax.all_gather(normed, TENSOR, axis=0, tiled=True)  78.6 us
    all_gather x1, waiting for transfers between devices, local(): down = lax.all_gather(down_weight, OWNERS, axis=1, tiled=True)  72.3 us
    all_to_all x1, blocking collectives, local(): lax.all_to_all(jnp.stack([grad] * lax.axis_size(TENSOR)), TENSOR, 0, 0)  39.9 us
    unnamed x1, blocking collectives  38.4 us
    reduce_scatter x1, waiting for transfers between devices, local(): lax.psum_scatter(jnp.dot(scaled, project_weight, preferred_element_type=j...  35.1 us
  transfers between devices with their start and end apart: 6, of which 6 were waited for; matrix products, arithmetic and copies ran while one was open for 4% of the time, Pallas kernels for 0%

profile of v1, /device:TPU:8, one launch (start us, length us, event | category | flops | bytes accessed | tf_op | source)
XLA Modules:
  0.0 617.1 jit_solution(15536174703729178731)
XLA Ops:
  7.2 1.1 fusion.5
  8.3 1.6 fusion.7
  10.0 2.0 pad_maximum_fusion
  12.1 0.7 all-gather.8.cloned.1.call-update
  12.9 4.4 convolution_convert_fusion.2
  17.3 78.6 %all-gather.4.cloned.1.call-done = bf16[256,3584]{1,0:T(8,128)(2,1)} async-done(((bf16[16,3584]{1,0:T(8,128)(2,1)}), bf16[256,3584]{1,0:T(8,128)(2,1)}) %all-gather.4.cloned.1.call-update) | async-done | bytes 1835024 | tf_op jit(solution)/shard_map/all_gather | solution.py:48
  96.0 112.9 %all-gather.6.cloned.1.call-done = bf16[3584,1184]{1,0:T(8,128)(2,1)} async-done(((bf16[224,1184]{1,0:T(8,128)(2,1)}), bf16[3584,1184]{1,0:T(8,128)(2,1)}) %all-gather.6.cloned.1.call-update) | async-done | bytes 8486928 | tf_op jit(solution)/shard_map/all_gather | solution.py:49
  208.9 7.8 %fusion.16 = f32[256,1184]{0,1:T(8,128)S(1)} fusion(bf16[256,3584]{1,0:T(8,128)(2,1)} %all-gather.4.cloned.1.call-done, bf16[3584,1184]{1,0:T(8,128)(2,1)} %all-gather.6.cloned.1.call-done), kind=kOutput, calls=%fused_computation.36 | convolution fusion | flops 2172649472 | bytes 11534336 | tf_op jit(solution)/shard_map/dot_general | solution.py:65
  216.9 72.3 %all-gather.8.cloned.1.call-done = bf16[592,3584]{0,1:T(8,128)(2,1)} async-done(((bf16[592,224]{0,1:T(8,128)(2,1)}), bf16[592,3584]{0,1:T(8,128)(2,1)}) %all-gather.8.cloned.1.call-update) | async-done | bytes 4243472 | tf_op jit(solution)/shard_map/all_gather | solution.py:52
  289.1 5.2 convolution_convert_fusion.1
  294.5 0.6 copy-done.8
  295.0 0.6 dynamic-slice
  296.4 38.4 %all-reduce = f32[256]{0:T(256)S(1)} all-reduce(f32[256]{0:T(256)S(1)} %fusion.2), channel_id=4, replica_groups=mesh['group'=2,'dp'=8,'tensor_0'=4,'tensor_1'=4] {'tensor_0','tensor_1'}, use_global_device_ids=true, to_apply=%region_6.7.clone | all-reduce | flops 256 | bytes 2048
  335.1 35.1 %reduce-scatter.6.cloned.1.call-done = bf16[16,3584]{1,0:T(8,128)(2,1)} async-done(((bf16[256,3584]{1,0:T(8,128)(2,1)}), bf16[16,3584]{1,0:T(8,128)(2,1)}) %reduce-scatter.6.cloned.1.call-update) | async-done | bytes 114704 | tf_op jit(solution)/shard_map/reduce_scatter | solution.py:58
  370.2 86.0 %reduce-scatter.4.cloned.1.call-done = bf16[16,3584]{1,0:T(8,128)(2,1)} async-done(((bf16[256,3584]{1,0:T(8,128)(2,1)}), bf16[16,3584]{1,0:T(8,128)(2,1)}) %reduce-scatter.4.cloned.1.call-update) | async-done | bytes 114704 | tf_op jit(solution)/shard_map/reduce_scatter | solution.py:68
  456.2 1.1 multiply_convert_fusion
  457.5 39.9 %all_to_all.14 = bf16[16,16,3584]{2,1,0:T(8,128)(2,1)S(1)} all-to-all(bf16[16,16,3584]{2,1,0:T(8,128)(2,1)S(1)} %stack.2), channel_id=1, replica_groups=mesh['group'=2,'dp'=8,'tensor_0'=4,'tensor_1'=4] {'tensor_0','tensor_1'}, dimensions={0} | all-to-all | bytes 3670016 | tf_op jit(solution)/shard_map/all_to_all | solution.py:78
  497.4 3.7 convolution_convert_fusion
  501.1 0.6 copy-done.7
  502.0 0.2 convolution_convert_fusion.3
  502.3 19.6 %all_to_all.15 = bf16[16,2,3584]{2,1,0:T(2,128)(2,1)S(1)} all-to-all(bf16[16,2,3584]{2,1,0:T(2,128)(2,1)S(1)} %all_to_all.9), channel_id=1, replica_groups=mesh['group'=2,'dp'=8,'tensor_0'=4,'tensor_1'=4] {'group','dp'}, dimensions={0} | all-to-all | bytes 458752 | tf_op jit(solution)/shard_map/all_to_all | solution.py:92
  521.9 0.8 broadcast_in_dim.18
  522.7 85.7 %reduce-scatter.8.cloned.1.call-done = bf16[224,592]{1,0:T(8,128)(2,1)} async-done(((bf16[3584,592]{1,0:T(8,128)(2,1)}), bf16[224,592]{1,0:T(8,128)(2,1)}) %reduce-scatter.8.cloned.1.call-update) | async-done | bytes 265232 | tf_op jit(solution)/shard_map/reduce_scatter | solution.py:80
  608.4 1.8 convert_element_type.76
  (37 shorter events, 1.5 us)
Async XLA Ops:
  7.2 5.7 copy-start.1
  7.2 5.7 copy-start.3
  7.2 88.8 %all-gather.4.cloned.1.call-start = ((), (), s32[]{:S(2)}) async-start(), calls=%async_computation.5 | async-start | bytes 1949696 | tf_op jit(solution)/shard_map/all_gather | solution.py:48
  10.0 198.9 %all-gather.6.cloned.1.call-start = ((), (), s32[]{:S(2)}) async-start(), calls=%async_computation.6 | async-start | bytes 9748480 | tf_op jit(solution)/shard_map/all_gather | solution.py:49
  12.1 277.1 %all-gather.8.cloned.1.call-start = ((), (), s32[]{:S(2)}) async-start(), calls=%async_computation.7 | async-start | bytes 4874240 | tf_op jit(solution)/shard_map/all_gather | solution.py:52
  12.8 357.4 %reduce-scatter.6.cloned.1.call-start = ((), (), s32[]{:S(2)}) async-start(), calls=%async_computation.9 | async-start | bytes 1949696 | tf_op jit(solution)/shard_map/reduce_scatter | solution.py:58
  17.3 438.9 %reduce-scatter.4.cloned.1.call-start = ((), (), s32[]{:S(2)}) async-start(), calls=%async_computation.8 | async-start | bytes 1949696 | tf_op jit(solution)/shard_map/reduce_scatter | solution.py:68
  294.4 0.7 copy-start.8
  294.4 40.5 %copy-start.4 = (f32[512]{0:T(512)S(1)}, f32[512]{0:T(512)}, u32[]{:S(2)}) copy-start(f32[512]{0:T(512)} %param.23) | copy-start | bytes 6148
  294.4 40.5 %copy-start.5 = (s32[16]{0:T(128)S(1)}, s32[16]{0:T(128)}, u32[]{:S(2)}) copy-start(s32[16]{0:T(128)} %param.21) | copy-start | bytes 196
  294.4 40.7 %copy-start.6 = (s32[16]{0:T(128)S(1)}, s32[16]{0:T(128)}, u32[]{:S(2)}) copy-start(s32[16]{0:T(128)} %param.22) | copy-start | bytes 196
  294.4 161.8 %copy-start = (bf16[16,3584]{1,0:T(8,128)(2,1)S(1)}, bf16[16,3584]{1,0:T(8,128)(2,1)}, u32[]{:S(2)}) copy-start(bf16[16,3584]{1,0:T(8,128)(2,1)} %param.15) | copy-start | bytes 344068
  294.4 314.0 %reduce-scatter.8.cloned.1.call-start = ((), (), s32[]{:S(2)}) async-start(), calls=%async_computation.10 | async-start | bytes 4874240 | tf_op jit(solution)/shard_map/reduce_scatter | solution.py:80
  501.1 0.7 copy-start.7
  501.1 0.9 copy-start.2
Sparse Core Ops, SparseCore 0:
  10.4 85.5 all-gather.3
  99.3 109.5 all-gather.5
  211.6 77.4 all-gather.7
  291.5 78.6 reduce-scatter.5
  372.8 83.3 reduce-scatter.3
  501.2 107.1 reduce-scatter.7
